TPU v7x, 256 devices: a whole 4x4x8 slice. The times are simulated.
256 devices in a mesh: row: 8 (over y, core), leaf: 32 (over x, z).
Axes of the slice: x: 4, y: 4, z: 8, core: 2. Of those that a mesh axis runs over, the one named last changes fastest.
Arguments:
- diag_blocks: float32 [32, 24, 256, 256], P('leaf', 'row'), as said below
- panel: float32 [32, 24, 768, 256], P('leaf', None, 'row'), may hold values from -1.5 to 1.5
- parent: int32 [32, 24, 1], replicated, may hold values from 0 to 31; in each aligned block of 24 rows (0 to 23, 24 to 47, ..., all dimensions but the last counted through in order) at most 2 rows name the same one
- rel: int32 [32, 24, 6], replicated, may hold values from 0 to 7, as said below
- front: float32 [32, 1024, 1024], P('leaf', None, 'row'), may hold values from -6 to 6
Outputs:
- factor_diag: float32 [32, 24, 256, 256], P('leaf', 'row')
- factor_panel: bfloat16 [32, 24, 768, 256], P('leaf', None, 'row')
- new_front: float32 [32, 1024, 1024], P('leaf', None, 'row')
Inputs may be any that keep to these rules, and one draw needn't show every extreme that they name: Among the 24 supernodes of one leaf index at most 2 have the same parent owner, and some leaf index reaches 2. `rel`: the 6 entries of each supernode name different blocks of the parent's front, in rising order. `diag_blocks`: every block is symmetric positive definite.
All inputs are finite; a program needn't handle non-finite values.
Results may differ from a plain program's by a relative error of at most 0.0011.
Values may be sent and summed in bfloat16 or wider, within the bound.
No kernel may reach another device: no remote copies, remote signals or barrier semaphores. Data moves between devices by JAX's collectives and lax.ppermute only.
A program may use at most 128 MiB of HBM per device.

v0:
```python
import jax
import jax.numpy as jnp
from jax import lax
from jax.sharding import PartitionSpec as P

W = 256
BS = 128
FB = 8
P_SIZE = 6


def on_device(diag_blocks, panel, parent, rel, front):
    row_count = lax.axis_size("row")
    leaf_count = lax.axis_size("leaf")
    row_index = lax.axis_index("row")
    leaf_index = lax.axis_index("leaf")
    own_factor = jnp.linalg.cholesky(diag_blocks[0])
    factors_all = lax.all_gather(own_factor, "row", axis=0, tiled=True)
    solved = jax.scipy.linalg.solve_triangular(
        factors_all, jnp.swapaxes(panel[0], 1, 2), lower=True
    )
    panel_rows = jnp.swapaxes(solved, 1, 2).astype(jnp.bfloat16)
    owners = parent[:, :, 0]
    supernodes = owners.shape[1]
    most_slots = max(2, 3 * supernodes // (2 * leaf_count))
    node_ids = jnp.arange(supernodes, dtype=jnp.int32)
    before = node_ids[None, :] < node_ids[:, None]
    same_owner = owners[:, :, None] == owners[:, None, :]
    position = jnp.sum(jnp.logical_and(same_owner, before[None]), axis=2)
    slot_ids = jnp.arange(most_slots, dtype=jnp.int32)
    targets = jnp.arange(leaf_count, dtype=jnp.int32)
    my_owner = lax.dynamic_index_in_dim(owners, leaf_index, 0, keepdims=False)
    my_position = lax.dynamic_index_in_dim(position, leaf_index, 0, keepdims=False)
    send_match = jnp.logical_and(
        my_owner[None, None, :] == targets[:, None, None],
        my_position[None, None, :] == slot_ids[None, :, None],
    )
    send_child = jnp.sum(jnp.where(send_match, node_ids, 0), axis=2)
    send_valid = jnp.any(send_match, axis=2)
    recv_match = jnp.logical_and(
        owners[:, None, :] == leaf_index, position[:, None, :] == slot_ids[None, :, None]
    )
    recv_valid = jnp.any(recv_match, axis=2)
    recv_blocks = jnp.sum(jnp.where(recv_match[..., None], rel[:, None, :, :], 0), axis=2)
    blocks_per_row = FB // row_count
    owned_blocks = row_index * blocks_per_row + jnp.arange(blocks_per_row, dtype=jnp.int32)
    columns = blocks_per_row * BS
    full_panel = lax.all_gather(panel_rows, "row", axis=1, tiled=True)
    my_blocks = lax.dynamic_index_in_dim(rel, leaf_index, 0, keepdims=False)
    leading = full_panel.shape[:-2]
    selector = (my_blocks[..., None, :] == owned_blocks[:, None]).astype(jnp.bfloat16)
    parted = full_panel.reshape(leading + (P_SIZE, BS, W))
    picked = jnp.einsum(
        "...tp,...pbw->...tbw", selector, parted, preferred_element_type=jnp.float32
    ).astype(jnp.bfloat16)
    picked = picked.reshape(leading + (columns, W))
    child_updates = jnp.einsum(
        "...iw,...cw->...ic", full_panel, picked, preferred_element_type=jnp.float32
    ).astype(jnp.bfloat16)
    outgoing = jnp.where(
        send_valid[..., None, None],
        jnp.take(child_updates, send_child, axis=0),
        jnp.zeros((), jnp.bfloat16),
    )
    incoming = lax.all_to_all(outgoing, "leaf", split_axis=0, concat_axis=0, tiled=True)
    front_ids = jnp.arange(FB, dtype=jnp.int32)
    placing = jnp.logical_and(
        recv_blocks[..., None, :] == front_ids[:, None], recv_valid[..., None, None]
    ).astype(jnp.bfloat16)
    parted_updates = incoming.reshape(incoming.shape[0], incoming.shape[1], P_SIZE, BS, columns)
    assembled = jnp.einsum(
        "smfp,smpic->fic", placing, parted_updates, preferred_element_type=jnp.float32
    )
    new_front = front[0] - assembled.reshape(FB * BS, columns)
    return (own_factor[None], panel_rows[None], new_front[None])


def solution(mesh):
    in_specs = (
        P("leaf", "row", None, None),
        P("leaf", None, "row", None),
        P(),
        P(),
        P("leaf", None, "row"),
    )
    out_specs = (P("leaf", "row", None, None), P("leaf", None, "row", None), P("leaf", None, "row"))
    return jax.shard_map(
        on_device, mesh=mesh, in_specs=in_specs, out_specs=out_specs, check_vma=False
    )
```

profile of v0, /device:TPU:7, one launch (start us, length us, event | category | flops | bytes accessed | tf_op | source)
XLA Modules:
  0.0 1081.7 jit_solution(9359395064277232795)
XLA Ops:
  7.2 0.0 all-gather.3.cloned.1.call-start
  7.3 1.4 copy.66
  8.7 1.2 fusion.16
  10.0 35.2 %custom-call.17 = f32[3,128,128]{2,1,0:T(8,128)S(1)} custom-call(f32[3,128,128]{2,1,0:T(8,128)S(1)} %cholesky.122), custom_call_target="Cholesky" | custom-call | tf_op jit(solution)/shard_map/jit(cholesky)/cholesky | solution.py:17
  45.2 29.5 %custom-call.18 = f32[3,1,128,128]{2,3,1,0:T(8,128)S(1)} custom-call(f32[3,1,128,128]{3,2,1,0:T(8,128)S(1)} %select_bitcast_fusion), custom_call_target="InvertDiagBlocksLowerTriangular" | custom-call | tf_op jit(solution)/shard_map/jit(cholesky)/cholesky | solution.py:17
  74.7 0.1 cholesky.117
  74.7 0.3 constant_dynamic-update-slice_fusion.1
  75.1 0.5 convolution_subtract_fusion
  75.6 35.2 %custom-call.19 = f32[3,128,128]{2,1,0:T(8,128)S(1)} custom-call(f32[3,128,128]{2,1,0:T(8,128)S(1)} %convolution_subtract_fusion), custom_call_target="Cholesky" | custom-call | tf_op jit(solution)/shard_map/jit(cholesky)/cholesky | solution.py:17
  110.8 0.1 compare_reduce_fusion
  111.0 1.0 select_select_fusion.1
  112.1 0.0 all-gather.3.cloned.1.call-update
  112.1 0.0 all-gather.5.cloned.1.call-start
  112.1 46.9 %all-gather.3.cloned.1.call-done = f32[24,256,256]{2,1,0:T(8,128)} async-done(((f32[3,256,256]{2,1,0:T(8,128)}), f32[24,256,256]{2,1,0:T(8,128)}) %all-gather.3.cloned.1.call-update) | async-done | bytes 6291472 | tf_op jit(solution)/shard_map/all_gather | solution.py:18
  159.0 6.3 broadcast_select_fusion
  165.4 0.1 triangular_solve.48
  165.4 0.0 copy-start.2
  165.4 10.5 while.1
  165.4 0.6 fusion.41
  166.0 5.0 bitcast_dynamic-update-slice_fusion.2
  171.0 0.6 fusion.41
  171.6 4.4 bitcast_dynamic-update-slice_fusion.2
  176.0 473.0 %custom-call.20 = f32[24,2,128,128]{2,3,1,0:T(8,128)} custom-call(f32[24,2,128,128]{3,2,1,0:T(8,128)} %bitcast.90), custom_call_target="InvertDiagBlocksLowerTriangular" | custom-call | tf_op jit(solution)/shard_map/jit(_solve_triangular)/vmap()/triangular_solve | solution.py:19
  649.0 0.0 copy-done.2
  649.0 2.9 fusion.32
  651.9 0.0 copy-start.1
  651.9 4.9 fusion.8
  656.9 0.0 copy-done.1
  656.9 1.5 fusion.11
  658.4 0.0 copy-start.5
  658.4 0.0 copy-start.4
  658.4 1.7 fusion.18
  660.2 0.0 all-gather.5.cloned.1.call-update
  660.2 0.0 copy-done.5
  660.2 0.2 convert_reduce_fusion
  660.4 0.2 dynamic-slice_reduce_fusion
  660.6 0.6 dynamic-slice_reduce_fusion.1
  661.2 0.1 iota_compare_fusion.5
  661.2 0.1 fusion.25
  661.3 0.1 copy.74
  661.5 0.1 and_reduce_fusion
  661.5 0.1 copy.73
  661.7 0.1 copy.76
  661.7 0.1 reshape.180
  661.9 0.0 copy-done.4
  661.9 0.1 constant_dynamic-slice_fusion.1
  662.0 0.1 copy.90
  662.1 0.1 copy.82
  662.2 54.8 %all-gather.5.cloned.1.call-done = bf16[24,768,256]{2,1,0:T(8,128)(2,1)} async-done(((bf16[24,96,256]{2,1,0:T(8,128)(2,1)}), bf16[24,768,256]{2,1,0:T(8,128)(2,1)}) %all-gather.5.cloned.1.call-update) | async-done | bytes 9437200 | tf_op jit(solution)/shard_map/all_gather | solution.py:48
  717.1 0.0 copy-start
  717.1 11.9 %fusion = bf16[24,1,128,256]{3,1,2,0:T(2,128)(2,1)} fusion(pred[24,6,1,1]{1,2,3,0:T(4,128)(4,1)S(1)} %copy.82, bf16[24,6,128,256]{3,2,1,0:T(8,128)(2,1)} %bitcast.84), kind=kOutput, calls=%fused_computation.3 | convolution fusion | flops 9437184 | bytes 11010192 | tf_op jit(solution)/shard_map/...tp,...pbw->...tbw/dot_general | solution.py:53
  729.0 0.0 copy-done
  729.0 6.1 convolution_convert_fusion
  735.1 9.5 gather_fusion
  744.6 11.0 %select_select_fusion = bf16[32,2,768,128]{3,2,1,0:T(8,128)(2,1)} fusion(bf16[32,2,768,128]{3,2,1,0:T(8,128)(2,1)} %bitcast.83, pred[32,2]{1,0:T(8,128)(4,1)S(1)} %copy.74, pred[32,2]{1,0:T(8,128)(4,1)S(1)} %copy.73), kind=kLoop, calls=%fused_computation.7 | loop fusion | flops 12582912 | bytes 25165952 | tf_op jit(solution)/shard_map/jit(_where)/select_n | solution.py:60
  755.6 9.7 all-to-all-start
  765.4 1.0 fusion.39
  766.4 294.6 %all-to-all-done = bf16[32,2,768,128]{3,2,1,0:T(8,128)(2,1)} async-done(((bf16[32,2,768,128]{3,2,1,0:T(8,128)(2,1)}), bf16[32,2,768,128]{3,2,1,0:T(8,128)(2,1)}, u32[]{:S(2)}, u32[]{:S(2)}) %all-to-all-start) | async-done | bytes 12582944 | tf_op jit(solution)/shard_map/all_to_all | solution.py:65
  1061.0 0.0 copy-start.3
  1061.0 12.8 %fusion.12 = f32[8,128,128]{2,0,1:T(8,128)S(1)} fusion(bf16[32,2,6,128,128]{4,3,2,1,0:T(8,128)(2,1)} %bitcast.24, s32[32,2,6]{0,2,1:T(8,128)S(1)} %select_reduce_fusion.2, pred[32,2]{0,1:T(4,128)(4,1)S(1)} %get-tuple-element.21), kind=kOutput, calls=%fused_computation.19 | convolution fusion | flops 100669440 | bytes 13108800 | tf_op jit(solution)/shard_map/smfp,smpic->fic/dot_general | solution.py:71
  1073.9 0.1 copy.78
  1074.0 0.0 copy-done.3
  1074.0 0.9 bitcast_subtract_fusion
  (20 shorter events, 0.3 us)
Async XLA Ops:
  7.2 151.9 %all-gather.3.cloned.1.call-start = ((), (), s32[]{:S(2)}) async-start(), calls=%async_computation.1 | async-start | bytes 7077888 | tf_op jit(solution)/shard_map/all_gather | solution.py:18
  112.1 605.0 %all-gather.5.cloned.1.call-start = ((), (), s32[]{:S(2)}) async-start(), calls=%async_computation.2 | async-start | bytes 10616832 | tf_op jit(solution)/shard_map/all_gather | solution.py:48
  165.4 483.5 %copy-start.2 = (f32[1,24,96,256]{3,2,1,0:T(8,128)S(1)}, f32[1,24,96,256]{3,2,1,0:T(8,128)}, u32[]{:S(2)}) copy-start(f32[1,24,96,256]{3,2,1,0:T(8,128)} %param.6) | copy-start | bytes 7077892
  651.9 5.0 copy-start.1
  658.4 1.8 copy-start.5
  658.4 3.4 copy-start.4
  717.1 11.9 %copy-start = (bf16[24,768,256]{2,1,0:T(8,128)(2,1)S(1)}, bf16[24,768,256]{2,1,0:T(8,128)(2,1)}, u32[]{:S(2)}) copy-start(bf16[24,768,256]{2,1,0:T(8,128)(2,1)} %all-gather.5.cloned.1.call-done) | copy-start | bytes 28311556
  755.6 305.4 %all-to-all-start = ((bf16[32,2,768,128]{3,2,1,0:T(8,128)(2,1)}), bf16[32,2,768,128]{3,2,1,0:T(8,128)(2,1)}, u32[]{:S(2)}, u32[]{:S(2)}) async-start(bf16[32,2,768,128]{3,2,1,0:T(8,128)(2,1)} %select_select_fusion), calls=%async_computation | async-start | bytes 25165824 | tf_op jit(solution)/shard_map/all_to_all | solution.py:65
  1061.0 12.9 %copy-start.3 = (f32[1,1024,128]{2,1,0:T(8,128)S(1)}, f32[1,1024,128]{2,1,0:T(8,128)}, u32[]{:S(2)}) copy-start(f32[1,1024,128]{2,1,0:T(8,128)} %param.9) | copy-start | bytes 1572868
Sparse Core Ops, SparseCore 0:
  112.2 46.8 all-gather.2
  660.3 56.7 all-gather.4
where the time goes:
time: 1090 us; the launch traced here: 1080 us
  other arithmetic  597 us (55%)
  waiting for transfers between devices  396 us (36%)
  matrix products  41.1 us (4%)
  local copies, waits for them, and re-layouts  23.2 us (2%)
  between operations  14.3 us (1%)
    another operation x3, other arithmetic, on_device(): jax.scipy.linalg.solve_triangular(factors_all, jnp.swapaxes(panel[0], 1,...  479 us
    all_to_all x1, waiting for transfers between devices, on_device(): lax.all_to_all(outgoing, 'leaf', split_axis=0, concat_axis=0, tiled=True)  295 us
    another operation x9, other arithmetic, on_device(): own_factor = jnp.linalg.cholesky(diag_blocks[0])  100 us
    all_gather x1, waiting for transfers between devices, on_device(): full_panel = lax.all_gather(panel_rows, 'row', axis=1, tiled=True)  54.8 us
    all_gather x1, waiting for transfers between devices, on_device(): factors_all = lax.all_gather(own_factor, 'row', axis=0, tiled=True)  46.9 us
  transfers between devices with their start and end apart: 3, of which 3 were waited for; matrix products, arithmetic and copies ran while one was open for 0% of the time, Pallas kernels for 0%

commit v1 on v0

v1 whole, which is shorter than its diff:
```python
import functools

import jax
import jax.numpy as jnp
from jax import lax
from jax.experimental import pallas as pl
from jax.experimental.pallas import tpu as pltpu
from jax.sharding import PartitionSpec as P

W = 256
BS = 128
FB = 8
P_SIZE = 6
K = 24
LEAVES = 32
ROWS = 8
OWN = K // ROWS
PANEL = P_SIZE * BS
PART = PANEL // ROWS
SLICE = W // ROWS
MOST = 2
SLOTS = LEAVES * MOST
NB = 64
HI = lax.Precision.HIGHEST
F32 = jnp.float32
BF16 = jnp.bfloat16

ANY = pl.BlockSpec(memory_space=pl.ANY)
VMEM = pl.BlockSpec(memory_space=pltpu.VMEM)
SMEM = pl.BlockSpec(memory_space=pltpu.SMEM)
PARAMS = pltpu.CompilerParams(vmem_limit_bytes=56 * 2**20)


def mm(a, b, trans_b=False):
    dims = (((1,), (1 if trans_b else 0,)), ((), ()))
    return lax.dot_general(a, b, dims, precision=HI, preferred_element_type=F32)


def eliminate(tiles, offset, nb):
    sub = lax.broadcasted_iota(jnp.int32, (8, 128), 0)
    for j in range(nb):
        first, jj = divmod(j, 8)
        lane = slice(offset + j, offset + j + 1)
        for ts in tiles:
            row = jnp.broadcast_to(ts[first][jj : jj + 1, :], (8, 128))
            pivot = jnp.broadcast_to(ts[first][jj : jj + 1, lane], (8, 128))
            scaled = row * (1.0 / pivot)
            for t in range(first, nb // 8):
                if t == first and jj == 7:
                    continue
                col = jnp.broadcast_to(ts[t][:, lane], (8, 128))
                if t == first:
                    col = jnp.where(sub > jj, col, 0.0)
                ts[t] = ts[t] - col * scaled
    return tiles


def factor_kernel(a_ref, l_ref, v_ref, s_ref):
    n, w = a_ref.shape[0], a_ref.shape[1]
    s_ref[...] = a_ref[...]
    lane = lax.broadcasted_iota(jnp.int32, (NB, 128), 1)
    sub = lax.broadcasted_iota(jnp.int32, (NB, 128), 0)
    for k in range(w // NB):
        lo, hi = k * NB, (k + 1) * NB
        off = lo % 128
        other = NB - off
        tile = slice(lo - off, lo - off + 128)
        own = (lane >= off) & (lane < off + NB)
        eye = (lane - other == sub).astype(F32)
        tiles = []
        for m in range(n):
            b = jnp.where(own, s_ref[m, lo:hi, tile], eye)
            tiles.append([b[8 * t : 8 * t + 8] for t in range(NB // 8)])
        tiles = eliminate(tiles, off, NB)
        for m in range(n):
            b = jnp.concatenate(tiles[m], axis=0)
            d = jnp.sum(jnp.where(lane - off == sub, b, 0.0), axis=1, keepdims=True)
            b = b * (1.0 / jnp.sqrt(d))
            up, inv = b[:, off : off + NB], b[:, other : other + NB]
            up = jnp.where(lane[:, :NB] >= sub[:, :NB], up, 0.0)
            inv = jnp.where(lane[:, :NB] <= sub[:, :NB], inv, 0.0)
            g = mm(inv, s_ref[m, lo:hi, :])
            left = [g[:, :lo]] if k else []
            right = [g[:, hi:]] if hi < w else []
            r = jnp.concatenate(left + [inv] + right, axis=1)
            col = lax.broadcasted_iota(jnp.int32, (NB, w), 1)
            v_ref[m, lo:hi, :] = jnp.where(col < hi, r, 0.0)
            zero = [jnp.zeros((NB, lo), F32)] if k else []
            ut = jnp.concatenate(zero + [up] + right, axis=1).T
            l_ref[m, :, lo:hi] = ut
            if hi < w:
                rest = s_ref[m, hi:, :]
                at = lax.broadcasted_iota(jnp.int32, rest.shape, 1)
                rest = jnp.where((at >= lo) & (at < hi), 0.0, rest)
                s_ref[m, hi:, :] = rest - mm(ut[hi:, :], r)


def factor(a):
    shape = jax.ShapeDtypeStruct(a.shape, F32)
    return pl.pallas_call(
        factor_kernel,
        out_shape=(shape, shape),
        in_specs=[VMEM],
        out_specs=(VMEM, VMEM),
        scratch_shapes=[pltpu.VMEM(a.shape, F32)],
        compiler_params=PARAMS,
        name="factor",
    )(a)


def split_kernel(r_ref, panel_ref, *refs):
    outs, sems = refs[:-1], refs[-1]
    copies = []
    for s in range(ROWS):
        to = lax.rem(r_ref[0] + s, ROWS)
        copies.append(
            pltpu.make_async_copy(panel_ref.at[pl.ds(to * OWN, OWN)], outs[s], sems.at[s])
        )
    for c in copies:
        c.start()
    for c in copies:
        c.wait()


def split(r, panel):
    piece = jax.ShapeDtypeStruct((OWN, PART, W), panel.dtype)
    return pl.pallas_call(
        split_kernel,
        out_shape=(piece,) * ROWS,
        in_specs=[SMEM, ANY],
        out_specs=(ANY,) * ROWS,
        scratch_shapes=[pltpu.SemaphoreType.DMA((ROWS,))],
        name="split",
    )(r, panel)


def join_kernel(r_ref, *refs):
    pieces, out_ref, sems = refs[:ROWS], refs[ROWS], refs[ROWS + 1]
    copies = []
    for s in range(ROWS):
        source = lax.rem(r_ref[0] + ROWS - s, ROWS)
        copies.append(
            pltpu.make_async_copy(pieces[s], out_ref.at[pl.ds(source * OWN, OWN)], sems.at[s])
        )
    for c in copies:
        c.start()
    for c in copies:
        c.wait()


def join(r, pieces):
    return pl.pallas_call(
        join_kernel,
        out_shape=jax.ShapeDtypeStruct((K,) + pieces[0].shape[1:], pieces[0].dtype),
        in_specs=[SMEM] + [ANY] * ROWS,
        out_specs=ANY,
        scratch_shapes=[pltpu.SemaphoreType.DMA((ROWS,))],
        name="join",
    )(r, *pieces)


def solve_kernel(r_ref, v_ref, *refs):
    pieces, xs, ts = refs[:ROWS], refs[ROWS : 2 * ROWS], refs[2 * ROWS : 3 * ROWS]
    p_ref, x_ref, t_ref, sems = refs[3 * ROWS :]
    r = r_ref[0]
    copies = []
    for s in range(ROWS):
        source = lax.rem(r + ROWS - s, ROWS)
        at = pl.ds(pl.multiple_of(source * PART, PART), PART)
        copies.append(pltpu.make_async_copy(pieces[s], p_ref.at[:, at], sems.at[s]))
    for c in copies:
        c.start()
    for c in copies:
        c.wait()
    one = lax.broadcasted_iota(jnp.int32, (W, W), 0) == lax.broadcasted_iota(jnp.int32, (W, W), 1)
    eye = one.astype(BF16)
    for m in range(OWN):
        x = mm(p_ref[m], v_ref[m], trans_b=True).astype(BF16)
        x_ref[m] = x
        t_ref[m] = lax.dot_general(
            eye, x, (((1,), (1,)), ((), ())), preferred_element_type=F32
        ).astype(BF16)
    for s in range(ROWS):
        to = lax.rem(r + s, ROWS)
        xs[s][...] = x_ref[:, pl.ds(pl.multiple_of(to * PART, PART), PART), :]
        ts[s][...] = t_ref[:, pl.ds(pl.multiple_of(to * SLICE, SLICE), SLICE), :]


def solve(r, inverse, pieces):
    row_piece = jax.ShapeDtypeStruct((OWN, PART, W), BF16)
    column_piece = jax.ShapeDtypeStruct((OWN, SLICE, PANEL), BF16)
    return pl.pallas_call(
        solve_kernel,
        out_shape=(row_piece,) * ROWS + (column_piece,) * ROWS,
        in_specs=[SMEM, VMEM] + [ANY] * ROWS,
        out_specs=(VMEM,) * (2 * ROWS),
        scratch_shapes=[
            pltpu.VMEM((OWN, PANEL, W), F32),
            pltpu.VMEM((OWN, PANEL, W), BF16),
            pltpu.VMEM((OWN, W, PANEL), BF16),
            pltpu.SemaphoreType.DMA((ROWS,)),
        ],
        compiler_params=PARAMS,
        name="solve",
    )(r, inverse, *pieces)


def outgoing_kernel(r_ref, owner_ref, *refs):
    pieces, out_ref = refs[:ROWS], refs[ROWS]
    used, place, sems = refs[ROWS + 1 :]
    for a in range(LEAVES):
        used[a] = 0
    for k in range(K):
        a = owner_ref[k]
        place[k] = MOST * a + used[a]
        used[a] = used[a] + 1
    copies = []
    for s in range(ROWS):
        source = lax.rem(r_ref[0] + ROWS - s, ROWS)
        for i in range(OWN):
            copies.append(
                pltpu.make_async_copy(
                    pieces[s].at[i], out_ref.at[place[source * OWN + i]], sems.at[s, i]
                )
            )
            copies[-1].start()
    for c in copies:
        c.wait()


def outgoing(r, owners, pieces):
    return pl.pallas_call(
        outgoing_kernel,
        out_shape=jax.ShapeDtypeStruct((SLOTS, SLICE, PANEL), BF16),
        in_specs=[SMEM, SMEM] + [ANY] * ROWS,
        out_specs=ANY,
        scratch_shapes=[
            pltpu.SMEM((LEAVES,), jnp.int32),
            pltpu.SMEM((K,), jnp.int32),
            pltpu.SemaphoreType.DMA((ROWS, OWN)),
        ],
        name="outgoing",
    )(r, owners, *pieces)


def children_kernel(leaf_ref, owner_ref, rel_ref, count_ref, slot_ref, block_ref):
    me = leaf_ref[0]

    def of_leaf(j, total):
        def of_node(k, carry):
            total, here = carry
            hit = owner_ref[j * K + k] == me

            @pl.when(hit)
            def _():
                slot_ref[total] = MOST * j + here
                for p in range(P_SIZE):
                    block_ref[total * P_SIZE + p] = rel_ref[(j * K + k) * P_SIZE + p]

            step = hit.astype(jnp.int32)
            return total + step, here + step

        return lax.fori_loop(0, K, of_node, (total, 0))[0]

    count_ref[0] = lax.fori_loop(0, LEAVES, of_leaf, 0)


def children(leaf, owners, rel):
    ints = lambda n: jax.ShapeDtypeStruct((n,), jnp.int32)
    return pl.pallas_call(
        children_kernel,
        out_shape=(ints(1), ints(SLOTS), ints(SLOTS * P_SIZE)),
        in_specs=[SMEM] * 3,
        out_specs=(SMEM,) * 3,
        name="children",
    )(leaf, owners, rel)


GROUP = 8
DEPTH = 2 * SLICE


def product_kernel(r_ref, count_ref, slot_ref, block_ref, a_ref, b_ref, *refs):
    outs = refs[:4]
    raw_ref, z_ref, acc_ref, sems = refs[4:]
    y, core = r_ref[0] // 2, lax.rem(r_ref[0], 2)
    count = count_ref[0]

    def fetch(i):
        slot = slot_ref[i]
        return (
            pltpu.make_async_copy(a_ref.at[slot], raw_ref.at[i, pl.ds(0, SLICE)], sems.at[i]),
            pltpu.make_async_copy(b_ref.at[slot], raw_ref.at[i, pl.ds(SLICE, SLICE)], sems.at[SLOTS + i]),
        )

    @pl.loop(0, count)
    def _(i):
        for c in fetch(i):
            c.start()

    acc_ref[...] = jnp.zeros_like(acc_ref)
    groups = (count + GROUP - 1) // GROUP

    @pl.loop(0, groups)
    def _(g):
        z_ref[...] = jnp.zeros_like(z_ref)
        for i in range(GROUP):
            n = g * GROUP + i

            @pl.when(n < count)
            def _():
                for c in fetch(n):
                    c.wait()
                for p in range(P_SIZE):
                    f = block_ref[n * P_SIZE + p]
                    at = lax.rem(f, 2) * 4 + f // 2
                    z_ref[i * DEPTH : (i + 1) * DEPTH, pl.ds(pl.multiple_of(at * BS, BS), BS)] = raw_ref[
                        n, :, p * BS : (p + 1) * BS
                    ]

        z = z_ref[...]
        half = z_ref[:, pl.ds(pl.multiple_of(core * 4 * BS, 4 * BS), 4 * BS)]
        acc_ref[...] += lax.dot_general(z, half, (((0,), (0,)), ((), ())), preferred_element_type=F32)

    for s in range(4):
        at = pl.ds(pl.multiple_of(lax.rem(y + s, 4) * BS, BS), BS)
        for place in range(FB):
            f = 2 * (place % 4) + place // 4
            outs[s][f * BS : (f + 1) * BS, :] = acc_ref[place * BS : (place + 1) * BS, at]


def product(r, count, slots, blocks, a, b):
    piece = jax.ShapeDtypeStruct((FB * BS, BS), F32)
    return pl.pallas_call(
        product_kernel,
        out_shape=(piece,) * 4,
        in_specs=[SMEM] * 4 + [ANY, ANY],
        out_specs=(VMEM,) * 4,
        scratch_shapes=[
            pltpu.VMEM((SLOTS, DEPTH, PANEL), BF16),
            pltpu.VMEM((GROUP * DEPTH, FB * BS), BF16),
            pltpu.VMEM((FB * BS, 4 * BS), F32),
            pltpu.SemaphoreType.DMA((2 * SLOTS,)),
        ],
        compiler_params=PARAMS,
        name="product",
    )(r, count, slots, blocks, a, b)


def shift_row(x, s):
    return lax.ppermute(x, "row", [(i, (i + s) % ROWS) for i in range(ROWS)])


def shift_y(x, s):
    return lax.ppermute(x, "row", [(i, (i + 2 * s) % ROWS) for i in range(ROWS)])


def swap_core(x):
    return lax.ppermute(x, "row", [(i, i ^ 1) for i in range(ROWS)])


def on_device(diag_blocks, panel, parent, rel, front):
    r = lax.axis_index("row").reshape(1)
    leaf = lax.axis_index("leaf").reshape(1)
    owners = parent.reshape(LEAVES * K)
    my_owners = lax.dynamic_slice(owners, (leaf[0] * K,), (K,))
    pieces = split(r, panel[0])
    pieces = [pieces[0]] + [shift_row(pieces[s], s) for s in range(1, ROWS)]
    factors, inverse = factor(diag_blocks[0])
    solved = solve(r, inverse, pieces)
    by_row, by_column = solved[:ROWS], solved[ROWS:]
    by_column = [by_column[0]] + [shift_row(by_column[s], s) for s in range(1, ROWS)]
    sent = outgoing(r, my_owners, by_column)
    by_row, sent, owners, rel = lax.optimization_barrier((by_row, sent, owners, rel))
    received = lax.all_to_all(
        sent.reshape(LEAVES, MOST, SLICE, PANEL), "leaf", split_axis=0, concat_axis=0, tiled=True
    ).reshape(SLOTS, SLICE, PANEL)
    by_row = [by_row[0]] + [shift_row(by_row[s], s) for s in range(1, ROWS)]
    factor_panel = join(r, by_row)
    count, slots, blocks = children(leaf, owners, rel.reshape(LEAVES * K * P_SIZE))
    other = swap_core(received)
    sums = product(r, count, slots, blocks, received, other)
    new_front = front[0] - sums[0]
    for s in range(1, 4):
        new_front = new_front - shift_y(sums[s], s)
    return (factors[None], factor_panel[None], new_front[None])


def solution(mesh):
    in_specs = (
        P("leaf", "row", None, None),
        P("leaf", None, "row", None),
        P(),
        P(),
        P("leaf", None, "row"),
    )
    out_specs = (P("leaf", "row", None, None), P("leaf", None, "row", None), P("leaf", None, "row"))
    return jax.shard_map(
        on_device, mesh=mesh, in_specs=in_specs, out_specs=out_specs, check_vma=False
    )
```

time: 1090 us -> 397 us (0.36)
  other arithmetic: 597 us -> 2.11 us
  waiting for transfers between devices: 396 us -> 53.1 us
  Pallas kernels: 0 us -> 221 us
  blocking collectives: 0 us -> 80.6 us
  matrix products: 41.1 us -> 0 us
  starting transfers between devices: 9.74 us -> 28.9 us
  local copies, waits for them, and re-layouts: 23.2 us -> 5.19 us
  between operations: 14.3 us -> 1.02 us
    another operation x12 -> x0, other arithmetic: 579 us -> none  [the longest x3 479 us: on_device(): jax.scipy.linalg.solve_triangular(factors_all, jnp.swapaxes(panel[0], 1,...]
    all_to_all x1 -> x0, waiting for transfers between devices: 295 us -> none  [on_device(): lax.all_to_all(outgoing, 'leaf', split_axis=0, concat_axis=0, tiled=True)]
    pallas_call x0 -> x7, Pallas kernels: none -> 221 us  [the longest x1 72.6 us: split(): pl.pallas_call(split_kernel, out_shape=(piece,) * ROWS, in_specs=[SMEM, A...]
    all_gather x2 -> x0, waiting for transfers between devices: 102 us -> none  [the longest x1 54.8 us: on_device(): full_panel = lax.all_gather(panel_rows, 'row', axis=1, tiled=True)]
    all_to_all x0 -> x1, blocking collectives: none -> 80.6 us  [on_device(): lax.all_to_all(sent.reshape(LEAVES, MOST, SLICE, PANEL), 'leaf', split_ax...]
    ppermute x0 -> x25, waiting for transfers between devices: none -> 53.1 us  [the longest x21 53.1 us: shift_row(): return lax.ppermute(x, 'row', [(i, (i + s) % ROWS) for i in range(ROWS)])]
    dot_general x3 -> x0, matrix products: 30.9 us -> none  [the longest x1 12.8 us: on_device(): jnp.einsum('smfp,smpic->fic', placing, parted_updates, preferred_element_...]
    ppermute x0 -> x25, starting transfers between devices: none -> 28.9 us  [the longest x21 24.6 us: shift_row(): return lax.ppermute(x, 'row', [(i, (i + s) % ROWS) for i in range(ROWS)])]
  transfers between devices with their start and end apart: 3 -> 25, of which waited for: 3 -> 11; matrix products, arithmetic and copies ran while one was open for 0% -> 1% of each run, Pallas kernels for 0% -> 26%
where the time goes in v1:
time: 397 us; the launch traced here: 392 us
  Pallas kernels  221 us (56%)
  blocking collectives  80.6 us (20%)
  waiting for transfers between devices  53.1 us (13%)
  starting transfers between devices  28.9 us (7%)
  local copies, waits for them, and re-layouts  5.19 us (1%)
    all_to_all x1, blocking collectives, on_device(): lax.all_to_all(sent.reshape(LEAVES, MOST, SLICE, PANEL), 'leaf', split_ax...  80.6 us
    pallas_call x1, Pallas kernels, split(): pl.pallas_call(split_kernel, out_shape=(piece,) * ROWS, in_specs=[SMEM, A...  72.6 us
    ppermute x21, waiting for transfers between devices, shift_row(): return lax.ppermute(x, 'row', [(i, (i + s) % ROWS) for i in range(ROWS)])  53.1 us
    pallas_call x1, Pallas kernels, factor(): pl.pallas_call(factor_kernel, out_shape=(shape, shape), in_specs=[VMEM],...  39.4 us
    pallas_call x1, Pallas kernels, outgoing(): pl.pallas_call(outgoing_kernel, out_shape=jax.ShapeDtypeStruct((SLOTS, SL...  37.8 us
    pallas_call x1, Pallas kernels, join(): pl.pallas_call(join_kernel, out_shape=jax.ShapeDtypeStruct((K,) + pieces[...  36.9 us
    ppermute x21, starting transfers between devices, shift_row(): return lax.ppermute(x, 'row', [(i, (i + s) % ROWS) for i in range(ROWS)])  24.6 us
    pallas_call x1, Pallas kernels, children(): pl.pallas_call(children_kernel, out_shape=(ints(1), ints(SLOTS), ints(SLO...  17.1 us
  transfers between devices with their start and end apart: 25, of which 11 were waited for; matrix products, arithmetic and copies ran while one was open for 1% of the time, Pallas kernels for 26%

profile of v1, /device:TPU:7, one launch (start us, length us, event | category | flops | bytes accessed | tf_op | source)
XLA Modules:
  0.0 391.5 jit_solution(14283243204906323579)
XLA Ops:
  0.6 72.6 %split.1 = (f32[3,96,256]{2,1,0:T(8,128)}, f32[3,96,256]{2,1,0:T(8,128)}, f32[3,96,256]{2,1,0:T(8,128)}, f32[3,96,256]{2,1,0:T(8,128)}, f32[3,96,256]{2,1,0:T(8,...) custom-call(s32[1]{0:T(128)} %bitcast.2.r_ref, f32[24,96,256]{2,1,0:T(8,128)} %bitcast.25), custom_call_target="tpu_custom_call" | custom-call | tf_op jit(solution)/shard_map/split/pallas_call | solution.py:127
  73.3 1.9 collective-permute-start
  75.2 1.3 collective-permute-start.1
  76.5 1.7 collective-permute-start.2
  78.2 0.3 collective-permute-start.3
  78.5 1.9 collective-permute-start.4
  80.5 1.2 collective-permute-done.refs_1_
  81.7 1.4 collective-permute-start.5
  83.1 6.7 %collective-permute-done.1.refs_2_ = f32[3,96,256]{2,1,0:T(8,128)S(1)} collective-permute-done((f32[3,96,256]{2,1,0:T(8,128)}, f32[3,96,256]{2,1,0:T(8,128)S(1)}, u32[]{:S(2)}, u32[]{:S(2)}) %collective-permute-start.1) | collective-permute-done | bytes 294944 | tf_op jit(solution)/shard_map/ppermute | solution.py:351
  89.7 0.0 collective-permute-start.6
  89.7 39.4 %factor.1 = (f32[3,256,256]{2,1,0:T(8,128)}, f32[3,256,256]{2,1,0:T(8,128)}) custom-call(f32[3,256,256]{2,1,0:T(8,128)} %bitcast.27), custom_call_target="tpu_custom_call" | custom-call | tf_op jit(solution)/shard_map/factor/pallas_call | solution.py:100
  129.1 0.0 collective-permute-done.2.refs_3_
  129.1 0.0 collective-permute-done.3.refs_4_
  129.2 0.0 collective-permute-done.4.refs_5_
  129.2 0.0 collective-permute-done.5.refs_6_
  129.2 0.0 collective-permute-done.6.refs_7_
  129.2 0.6 copy-done.3
  129.9 0.1 copy-done.4
  130.0 0.1 copy-done.5
  130.1 0.1 copy-done.6
  130.2 0.1 copy-done.7
  130.3 8.2 %solve.1 = (bf16[3,96,256]{2,1,0:T(8,128)(2,1)}, bf16[3,96,256]{2,1,0:T(8,128)(2,1)}, bf16[3,96,256]{2,1,0:T(8,128)(2,1)}, bf16[3,96,256]{2,1,0:T(8,128)(2,1)}, ...) custom-call(s32[1]{0:T(128)} %bitcast.2.r_ref, ...), custom_call_target="tpu_custom_call" | custom-call | tf_op jit(solution)/shard_map/solve/pallas_call | solution.py:192
  138.4 1.6 collective-permute-start.7
  140.1 0.4 collective-permute-start.8
  140.5 2.1 collective-permute-start.9
  142.5 1.7 collective-permute-start.10
  144.3 2.6 collective-permute-start.11
  146.9 0.0 collective-permute-done.7.refs_1_
  146.9 9.4 %collective-permute-done.8.refs_2_ = bf16[3,32,768]{2,1,0:T(8,128)(2,1)S(1)} collective-permute-done((bf16[3,32,768]{2,1,0:T(8,128)(2,1)}, bf16[3,32,768]{2,1,0:T(8,128)(2,1)S(1)}, u32[]{:S(2)}, u32[]{:S(2)}) %collective-permute-start.8) | collective-permute-done | bytes 147488 | tf_op jit(solution)/shard_map/ppermute | solution.py:351
  156.3 0.0 collective-permute-start.13
  156.3 0.1 copy.8
  156.4 0.1 reshape.25.owner_ref
  156.5 0.6 dynamic_slice.3.owner_ref
  157.0 0.0 collective-permute-done.9.refs_3_
  157.1 0.0 collective-permute-done.10.refs_4_
  157.1 0.1 collective-permute-done.12.refs_6_
  157.2 3.9 collective-permute-done.13.refs_7_
  161.1 0.6 copy-done.15
  161.7 37.8 %outgoing.1 = bf16[64,32,768]{2,1,0:T(8,128)(2,1)} custom-call(s32[1]{0:T(128)} %bitcast.2.r_ref, s32[24]{0:T(128)} %dynamic_slice.3.owner_ref, bf16[3,32,768]{2,1,0:T(8,128)(2,1)} %get-tuple-element.65.refs_0_, bf16[3,32,768]{2,1,0:T(8,128)(2,1)} %copy-done.8, bf16[3,32,768]{2,1,0:T(8,128)(2,1)} %copy-done.9, bf16[3,32,768]{2,1,0:T(8,128)(2,1)} %copy-done.10, ...), custom_call_target="tpu_custom_call" | custom-call | tf_op jit(solution)/shard_map/outgoing/pallas_call | solution.py:232
  199.6 80.6 %all_to_all.5 = bf16[32,2,32,768]{3,2,1,0:T(8,128)(2,1)S(1)} all-to-all(bf16[32,2,32,768]{3,2,1,0:T(8,128)(2,1)} %bitcast.24), channel_id=1, replica_groups=mesh['row'=8,'leaf'=32] {'leaf'}, dimensions={0} | all-to-all | bytes 6291456 | tf_op jit(solution)/shard_map/all_to_all | solution.py:375
  280.2 0.0 collective-permute-start.21
  280.2 0.0 collective-permute-start.14
  280.2 1.2 copy.9
  281.4 0.9 reshape.27.rel_ref
  282.3 17.1 %children.1 = (s32[1]{0:T(128)}, s32[64]{0:T(128)}, s32[384]{0:T(512)}) custom-call(s32[1]{0:T(128)} %bitcast.6.leaf_ref, s32[768]{0:T(1024)} %copy-done.21, s32[4608]{0:T(1024)} %reshape.27.rel_ref), custom_call_target="tpu_custom_call" | custom-call | tf_op jit(solution)/shard_map/children/pallas_call | solution.py:270
  299.4 8.5 %product.1 = (f32[1024,128]{1,0:T(8,128)}, f32[1024,128]{1,0:T(8,128)}, f32[1024,128]{1,0:T(8,128)}, f32[1024,128]{1,0:T(8,128)}) custom-call(s32[1]{0:T(128)} %bitcast.2.r_ref, s32[1]{0:T(128)} %get-tuple-element.83.count_ref, s32[64]{0:T(128)} %get-tuple-element.84.slot_ref, s32[384]{0:T(512)} %get-tuple-element.85.block_ref, ...), custom_call_target="tpu_custom_call" | custom-call | tf_op jit(solution)/shard_map/product/pallas_call | solution.py:334
  308.0 0.1 collective-permute-start.22
  308.1 4.1 %collective-permute-start.23 = (f32[1024,128]{1,0:T(8,128)}, f32[1024,128]{1,0:T(8,128)S(1)}, u32[]{:S(2)}, u32[]{:S(2)}) collective-permute-start(f32[1024,128]{1,0:T(8,128)} %get-tuple-element.89), channel_id=1, source_target_pairs={{0,128},{32,160},{64,192},{96,224},{128,0},{160,32},{192,64},{224,... | collective-permute-start | bytes 1572872 | tf_op jit(solution)/shard_map/ppermute | solution.py:355
  312.2 0.0 collective-permute-start.24
  312.3 1.4 collective-permute-start.15
  313.7 0.7 collective-permute-start.16
  314.4 23.3 %collective-permute-done.15.refs_2_ = bf16[3,96,256]{2,1,0:T(8,128)(2,1)S(1)} collective-permute-done((bf16[3,96,256]{2,1,0:T(8,128)(2,1)S(1)}, bf16[3,96,256]{2,1,0:T(8,128)(2,1)S(1)}, u32[]{:S(2)}, u32[]{:S(2)}) %collective-permute-start.15) | collective-permute-done | bytes 147488 | tf_op jit(solution)/shard_map/ppermute | solution.py:351
  337.6 2.6 collective-permute-start.17
  340.2 0.9 collective-permute-done.16.refs_3_
  341.1 2.4 collective-permute-done.17.refs_4_
  343.6 2.9 collective-permute-start.19
  346.5 0.8 collective-permute-done.18.refs_5_
  347.2 2.6 collective-permute-done.19.refs_6_
  349.8 1.9 collective-permute-done.20.refs_7_
  351.8 0.7 copy-done.20
  352.5 36.9 %join.1 = bf16[24,96,256]{2,1,0:T(8,128)(2,1)} custom-call(s32[1]{0:T(128)} %bitcast.2.r_ref, bf16[3,96,256]{2,1,0:T(8,128)(2,1)} %get-tuple-element.73.refs_0_, bf16[3,96,256]{2,1,0:T(8,128)(2,1)} %collective-permute-done.14.refs_1_, bf16[3,96,256]{2,1,0:T(8,128)(2,1)} %copy-done.14, bf16[3,96,256]{2,1,0:T(8,128)(2,1)} %copy-done.16, ...), custom_call_target="tpu_custom_call" | custom-call | tf_op jit(solution)/shard_map/join/pallas_call | solution.py:152
  389.4 0.0 collective-permute-done.22
  389.4 0.0 collective-permute-done.24
  389.4 2.1 fusion.3
  (58 shorter events, 0.1 us)
Async XLA Ops:
  0.6 155.6 %copy-start.22 = (s32[32,24,1]{0,2,1:T(1,128)S(1)}, s32[32,24,1]{0,2,1:T(1,128)}, u32[]{:S(2)}) copy-start(s32[32,24,1]{0,2,1:T(1,128)} %param.7) | copy-start | bytes 9220
  73.3 8.4 %collective-permute-start = (f32[3,96,256]{2,1,0:T(8,128)}, f32[3,96,256]{2,1,0:T(8,128)S(1)}, u32[]{:S(2)}, u32[]{:S(2)}) collective-permute-start(f32[3,96,256]{2,1,0:T(8,128)} %get-tuple-element.50), channel_id=1, source_target_pairs={{0,32},{32,64},{64,96},{96,128},{128,160},{160,192},{192,224},{224... | collective-permute-start | bytes 884744 | tf_op jit(solution)/shard_map/ppermute | solution.py:351
  75.2 14.6 %collective-permute-start.1 = (f32[3,96,256]{2,1,0:T(8,128)}, f32[3,96,256]{2,1,0:T(8,128)S(1)}, u32[]{:S(2)}, u32[]{:S(2)}) collective-permute-start(f32[3,96,256]{2,1,0:T(8,128)} %get-tuple-element.51), channel_id=1, source_target_pairs={{0,64},{32,96},{64,128},{96,160},{128,192},{160,224},{192,0},{224,... | collective-permute-start | bytes 884744 | tf_op jit(solution)/shard_map/ppermute | solution.py:351
  76.5 52.7 %collective-permute-start.2 = (f32[3,96,256]{2,1,0:T(8,128)}, f32[3,96,256]{2,1,0:T(8,128)S(1)}, u32[]{:S(2)}, u32[]{:S(2)}) collective-permute-start(f32[3,96,256]{2,1,0:T(8,128)} %get-tuple-element.52), channel_id=1, source_target_pairs={{0,96},{32,128},{64,160},{96,192},{128,224},{160,0},{192,32},{224,... | collective-permute-start | bytes 884744 | tf_op jit(solution)/shard_map/ppermute | solution.py:351
  78.2 51.0 %collective-permute-start.3 = (f32[3,96,256]{2,1,0:T(8,128)}, f32[3,96,256]{2,1,0:T(8,128)S(1)}, u32[]{:S(2)}, u32[]{:S(2)}) collective-permute-start(f32[3,96,256]{2,1,0:T(8,128)} %get-tuple-element.53), channel_id=1, source_target_pairs={{0,128},{32,160},{64,192},{96,224},{128,0},{160,32},{192,64},{224,... | collective-permute-start | bytes 884744 | tf_op jit(solution)/shard_map/ppermute | solution.py:351
  78.5 50.6 %collective-permute-start.4 = (f32[3,96,256]{2,1,0:T(8,128)}, f32[3,96,256]{2,1,0:T(8,128)S(1)}, u32[]{:S(2)}, u32[]{:S(2)}) collective-permute-start(f32[3,96,256]{2,1,0:T(8,128)} %get-tuple-element.54), channel_id=1, source_target_pairs={{0,160},{32,192},{64,224},{96,0},{128,32},{160,64},{192,96},{224,1... | collective-permute-start | bytes 884744 | tf_op jit(solution)/shard_map/ppermute | solution.py:351
  81.7 47.5 %copy-start.1 = (f32[3,96,256]{2,1,0:T(8,128)}, f32[3,96,256]{2,1,0:T(8,128)S(1)}, u32[]{:S(2)}) copy-start(f32[3,96,256]{2,1,0:T(8,128)S(1)} %collective-permute-done.refs_1_) | copy-start | bytes 884740
  81.7 47.5 %collective-permute-start.5 = (f32[3,96,256]{2,1,0:T(8,128)}, f32[3,96,256]{2,1,0:T(8,128)S(1)}, u32[]{:S(2)}, u32[]{:S(2)}) collective-permute-start(f32[3,96,256]{2,1,0:T(8,128)} %get-tuple-element.55), channel_id=1, source_target_pairs={{0,192},{32,224},{64,0},{96,32},{128,64},{160,96},{192,128},{224,1... | collective-permute-start | bytes 884744 | tf_op jit(solution)/shard_map/ppermute | solution.py:351
  89.7 39.5 %copy-start.2 = (f32[3,96,256]{2,1,0:T(8,128)}, f32[3,96,256]{2,1,0:T(8,128)S(1)}, u32[]{:S(2)}) copy-start(f32[3,96,256]{2,1,0:T(8,128)S(1)} %collective-permute-done.1.refs_2_) | copy-start | bytes 884740
  89.7 39.5 %collective-permute-start.6 = (f32[3,96,256]{2,1,0:T(8,128)}, f32[3,96,256]{2,1,0:T(8,128)S(1)}, u32[]{:S(2)}, u32[]{:S(2)}) collective-permute-start(f32[3,96,256]{2,1,0:T(8,128)} %get-tuple-element.56), channel_id=1, source_target_pairs={{0,224},{32,0},{64,32},{96,64},{128,96},{160,128},{192,160},{224,1... | collective-permute-start | bytes 884744 | tf_op jit(solution)/shard_map/ppermute | solution.py:351
  129.1 0.7 copy-start.3
  129.2 0.8 copy-start.4
  129.2 0.9 copy-start.5
  129.2 1.0 copy-start.6
  129.2 1.0 copy-start.7
  138.4 8.5 %collective-permute-start.7 = (bf16[3,32,768]{2,1,0:T(8,128)(2,1)}, bf16[3,32,768]{2,1,0:T(8,128)(2,1)S(1)}, u32[]{:S(2)}, u32[]{:S(2)}) collective-permute-start(bf16[3,32,768]{2,1,0:T(8,128)(2,1)} %get-tuple-element.66), channel_id=1, source_target_pairs={{0,32},{32,64},{64,96},{96,128},{128,160},{160,192},{192,224},{224... | collective-permute-start | bytes 442376 | tf_op jit(solution)/shard_map/ppermute | solution.py:351
  140.1 16.2 %collective-permute-start.8 = (bf16[3,32,768]{2,1,0:T(8,128)(2,1)}, bf16[3,32,768]{2,1,0:T(8,128)(2,1)S(1)}, u32[]{:S(2)}, u32[]{:S(2)}) collective-permute-start(bf16[3,32,768]{2,1,0:T(8,128)(2,1)} %get-tuple-element.67), channel_id=1, source_target_pairs={{0,64},{32,96},{64,128},{96,160},{128,192},{160,224},{192,0},{224,... | collective-permute-start | bytes 442376 | tf_op jit(solution)/shard_map/ppermute | solution.py:351
  140.5 16.6 %collective-permute-start.9 = (bf16[3,32,768]{2,1,0:T(8,128)(2,1)}, bf16[3,32,768]{2,1,0:T(8,128)(2,1)S(1)}, u32[]{:S(2)}, u32[]{:S(2)}) collective-permute-start(bf16[3,32,768]{2,1,0:T(8,128)(2,1)} %get-tuple-element.68), channel_id=1, source_target_pairs={{0,96},{32,128},{64,160},{96,192},{128,224},{160,0},{192,32},{224,... | collective-permute-start | bytes 442376 | tf_op jit(solution)/shard_map/ppermute | solution.py:351
  142.5 14.5 %collective-permute-start.10 = (bf16[3,32,768]{2,1,0:T(8,128)(2,1)}, bf16[3,32,768]{2,1,0:T(8,128)(2,1)S(1)}, u32[]{:S(2)}, u32[]{:S(2)}) collective-permute-start(bf16[3,32,768]{2,1,0:T(8,128)(2,1)} %get-tuple-element.69), channel_id=1, source_target_pairs={{0,128},{32,160},{64,192},{96,224},{128,0},{160,32},{192,64},{224,... | collective-permute-start | bytes 442376 | tf_op jit(solution)/shard_map/ppermute | solution.py:351
  144.3 12.8 %collective-permute-start.11 = (bf16[3,32,768]{2,1,0:T(8,128)(2,1)}, bf16[3,32,768]{2,1,0:T(8,128)(2,1)S(1)}, u32[]{:S(2)}, u32[]{:S(2)}) collective-permute-start(bf16[3,32,768]{2,1,0:T(8,128)(2,1)} %get-tuple-element.70), channel_id=1, source_target_pairs={{0,160},{32,192},{64,224},{96,0},{128,32},{160,64},{192,96},{224,1... | collective-permute-start | bytes 442376 | tf_op jit(solution)/shard_map/ppermute | solution.py:351
  146.9 14.1 %copy-start.8 = (bf16[3,32,768]{2,1,0:T(8,128)(2,1)}, bf16[3,32,768]{2,1,0:T(8,128)(2,1)S(1)}, u32[]{:S(2)}) copy-start(bf16[3,32,768]{2,1,0:T(8,128)(2,1)S(1)} %collective-permute-done.7.refs_1_) | copy-start | bytes 442372
  146.9 10.2 %collective-permute-start.12 = (bf16[3,32,768]{2,1,0:T(8,128)(2,1)}, bf16[3,32,768]{2,1,0:T(8,128)(2,1)S(1)}, u32[]{:S(2)}, u32[]{:S(2)}) collective-permute-start(bf16[3,32,768]{2,1,0:T(8,128)(2,1)} %get-tuple-element.71), channel_id=1, source_target_pairs={{0,192},{32,224},{64,0},{96,32},{128,64},{160,96},{192,128},{224,1... | collective-permute-start | bytes 442376 | tf_op jit(solution)/shard_map/ppermute | solution.py:351
  156.3 4.8 %copy-start.9 = (bf16[3,32,768]{2,1,0:T(8,128)(2,1)}, bf16[3,32,768]{2,1,0:T(8,128)(2,1)S(1)}, u32[]{:S(2)}) copy-start(bf16[3,32,768]{2,1,0:T(8,128)(2,1)S(1)} %collective-permute-done.8.refs_2_) | copy-start | bytes 442372
  156.3 4.8 %collective-permute-start.13 = (bf16[3,32,768]{2,1,0:T(8,128)(2,1)}, bf16[3,32,768]{2,1,0:T(8,128)(2,1)S(1)}, u32[]{:S(2)}, u32[]{:S(2)}) collective-permute-start(bf16[3,32,768]{2,1,0:T(8,128)(2,1)} %get-tuple-element.72), channel_id=1, source_target_pairs={{0,224},{32,0},{64,32},{96,64},{128,96},{160,128},{192,160},{224,1... | collective-permute-start | bytes 442376 | tf_op jit(solution)/shard_map/ppermute | solution.py:351
  156.4 123.7 %copy-start.21 = (s32[768]{0:T(1024)}, s32[768]{0:T(1024)S(1)}, u32[]{:S(2)}) copy-start(s32[768]{0:T(1024)S(1)} %reshape.25.owner_ref) | copy-start | bytes 9220
  157.1 4.0 %copy-start.10 = (bf16[3,32,768]{2,1,0:T(8,128)(2,1)}, bf16[3,32,768]{2,1,0:T(8,128)(2,1)S(1)}, u32[]{:S(2)}) copy-start(bf16[3,32,768]{2,1,0:T(8,128)(2,1)S(1)} %collective-permute-done.9.refs_3_) | copy-start | bytes 442372
  157.1 4.0 %copy-start.11 = (bf16[3,32,768]{2,1,0:T(8,128)(2,1)}, bf16[3,32,768]{2,1,0:T(8,128)(2,1)S(1)}, u32[]{:S(2)}) copy-start(bf16[3,32,768]{2,1,0:T(8,128)(2,1)S(1)} %collective-permute-done.10.refs_4_) | copy-start | bytes 442372
  157.1 4.0 %copy-start.12 = (bf16[3,32,768]{2,1,0:T(8,128)(2,1)}, bf16[3,32,768]{2,1,0:T(8,128)(2,1)S(1)}, u32[]{:S(2)}) copy-start(bf16[3,32,768]{2,1,0:T(8,128)(2,1)S(1)} %collective-permute-done.11.refs_5_) | copy-start | bytes 442372
  157.2 3.9 %copy-start.13 = (bf16[3,32,768]{2,1,0:T(8,128)(2,1)}, bf16[3,32,768]{2,1,0:T(8,128)(2,1)S(1)}, u32[]{:S(2)}) copy-start(bf16[3,32,768]{2,1,0:T(8,128)(2,1)S(1)} %collective-permute-done.12.refs_6_) | copy-start | bytes 442372
  161.1 0.7 copy-start.15
  280.2 19.2 %copy-start = (bf16[32,2,32,768]{3,2,1,0:T(8,128)(2,1)}, bf16[32,2,32,768]{3,2,1,0:T(8,128)(2,1)S(1)}, u32[]{:S(2)}) copy-start(bf16[32,2,32,768]{3,2,1,0:T(8,128)(2,1)S(1)} %all_to_all.5) | copy-start | bytes 9437188
  280.2 19.2 %collective-permute-start.21 = (bf16[64,32,768]{2,1,0:T(8,128)(2,1)S(1)}, bf16[64,32,768]{2,1,0:T(8,128)(2,1)}, u32[]{:S(2)}, u32[]{:S(2)}) collective-permute-start(bf16[64,32,768]{2,1,0:T(8,128)(2,1)S(1)} %bitcast.22), channel_id=1, source_target_pairs={{0,32},{32,0},{64,96},{96,64},{128,160},{160,128},{192,224},{224,1... | collective-permute-start | bytes 9437192 | tf_op jit(solution)/shard_map/ppermute | solution.py:359
  280.2 33.5 %collective-permute-start.14 = (bf16[3,96,256]{2,1,0:T(8,128)(2,1)}, bf16[3,96,256]{2,1,0:T(8,128)(2,1)}, u32[]{:S(2)}, u32[]{:S(2)}) collective-permute-start(bf16[3,96,256]{2,1,0:T(8,128)(2,1)} %get-tuple-element.74), channel_id=1, source_target_pairs={{0,32},{32,64},{64,96},{96,128},{128,160},{160,192},{192,224},{224... | collective-permute-start | bytes 442376 | tf_op jit(solution)/shard_map/ppermute | solution.py:351
  299.4 12.9 %copy-start.28 = (bf16[3,96,256]{2,1,0:T(8,128)(2,1)S(1)}, bf16[3,96,256]{2,1,0:T(8,128)(2,1)}, u32[]{:S(2)}) copy-start(bf16[3,96,256]{2,1,0:T(8,128)(2,1)} %get-tuple-element.75) | copy-start | bytes 442372
  299.4 14.3 %copy-start.27 = (bf16[3,96,256]{2,1,0:T(8,128)(2,1)S(1)}, bf16[3,96,256]{2,1,0:T(8,128)(2,1)}, u32[]{:S(2)}) copy-start(bf16[3,96,256]{2,1,0:T(8,128)(2,1)} %get-tuple-element.76) | copy-start | bytes 442372
  299.4 38.2 %copy-start.26 = (bf16[3,96,256]{2,1,0:T(8,128)(2,1)S(1)}, bf16[3,96,256]{2,1,0:T(8,128)(2,1)}, u32[]{:S(2)}) copy-start(bf16[3,96,256]{2,1,0:T(8,128)(2,1)} %get-tuple-element.77) | copy-start | bytes 442372
  299.4 41.7 %copy-start.25 = (bf16[3,96,256]{2,1,0:T(8,128)(2,1)S(1)}, bf16[3,96,256]{2,1,0:T(8,128)(2,1)}, u32[]{:S(2)}) copy-start(bf16[3,96,256]{2,1,0:T(8,128)(2,1)} %get-tuple-element.78) | copy-start | bytes 442372
  299.4 44.1 %copy-start.24 = (bf16[3,96,256]{2,1,0:T(8,128)(2,1)S(1)}, bf16[3,96,256]{2,1,0:T(8,128)(2,1)}, u32[]{:S(2)}) copy-start(bf16[3,96,256]{2,1,0:T(8,128)(2,1)} %get-tuple-element.79) | copy-start | bytes 442372
  299.4 47.8 %copy-start.23 = (bf16[3,96,256]{2,1,0:T(8,128)(2,1)S(1)}, bf16[3,96,256]{2,1,0:T(8,128)(2,1)}, u32[]{:S(2)}) copy-start(bf16[3,96,256]{2,1,0:T(8,128)(2,1)} %get-tuple-element.80) | copy-start | bytes 442372
  308.0 81.4 %collective-permute-start.22 = (f32[1024,128]{1,0:T(8,128)}, f32[1024,128]{1,0:T(8,128)S(1)}, u32[]{:S(2)}, u32[]{:S(2)}) collective-permute-start(f32[1024,128]{1,0:T(8,128)} %get-tuple-element.88), channel_id=1, source_target_pairs={{0,64},{32,96},{64,128},{96,160},{128,192},{160,224},{192,0},{224,... | collective-permute-start | bytes 1572872 | tf_op jit(solution)/shard_map/ppermute | solution.py:355
  308.1 81.3 %collective-permute-start.23 = (f32[1024,128]{1,0:T(8,128)}, f32[1024,128]{1,0:T(8,128)S(1)}, u32[]{:S(2)}, u32[]{:S(2)}) collective-permute-start(f32[1024,128]{1,0:T(8,128)} %get-tuple-element.89), channel_id=1, source_target_pairs={{0,128},{32,160},{64,192},{96,224},{128,0},{160,32},{192,64},{224,... | collective-permute-start | bytes 1572872 | tf_op jit(solution)/shard_map/ppermute | solution.py:355
  312.2 77.2 %collective-permute-start.24 = (f32[1024,128]{1,0:T(8,128)}, f32[1024,128]{1,0:T(8,128)S(1)}, u32[]{:S(2)}, u32[]{:S(2)}) collective-permute-start(f32[1024,128]{1,0:T(8,128)} %get-tuple-element.90), channel_id=1, source_target_pairs={{0,192},{32,224},{64,0},{96,32},{128,64},{160,96},{192,128},{224,1... | collective-permute-start | bytes 1572872 | tf_op jit(solution)/shard_map/ppermute | solution.py:355
  312.3 25.3 %collective-permute-start.15 = (bf16[3,96,256]{2,1,0:T(8,128)(2,1)S(1)}, bf16[3,96,256]{2,1,0:T(8,128)(2,1)S(1)}, u32[]{:S(2)}, u32[]{:S(2)}) collective-permute-start(bf16[3,96,256]{2,1,0:T(8,128)(2,1)S(1)} %copy-done.28), channel_id=1, source_target_pairs={{0,64},{32,96},{64,128},{96,160},{128,192},{160,224},{192,0},{224,... | collective-permute-start | bytes 442376 | tf_op jit(solution)/shard_map/ppermute | solution.py:351
  313.7 27.4 %collective-permute-start.16 = (bf16[3,96,256]{2,1,0:T(8,128)(2,1)S(1)}, bf16[3,96,256]{2,1,0:T(8,128)(2,1)S(1)}, u32[]{:S(2)}, u32[]{:S(2)}) collective-permute-start(bf16[3,96,256]{2,1,0:T(8,128)(2,1)S(1)} %copy-done.27), channel_id=1, source_target_pairs={{0,96},{32,128},{64,160},{96,192},{128,224},{160,0},{192,32},{224,... | collective-permute-start | bytes 442376 | tf_op jit(solution)/shard_map/ppermute | solution.py:351
  337.6 14.2 %copy-start.14 = (bf16[3,96,256]{2,1,0:T(8,128)(2,1)}, bf16[3,96,256]{2,1,0:T(8,128)(2,1)S(1)}, u32[]{:S(2)}) copy-start(bf16[3,96,256]{2,1,0:T(8,128)(2,1)S(1)} %collective-permute-done.15.refs_2_) | copy-start | bytes 442372
  337.6 5.9 %collective-permute-start.17 = (bf16[3,96,256]{2,1,0:T(8,128)(2,1)S(1)}, bf16[3,96,256]{2,1,0:T(8,128)(2,1)S(1)}, u32[]{:S(2)}, u32[]{:S(2)}) collective-permute-start(bf16[3,96,256]{2,1,0:T(8,128)(2,1)S(1)} %copy-done.26), channel_id=1, source_target_pairs={{0,128},{32,160},{64,192},{96,224},{128,0},{160,32},{192,64},{224,... | collective-permute-start | bytes 442376 | tf_op jit(solution)/shard_map/ppermute | solution.py:351
  341.1 10.7 %copy-start.16 = (bf16[3,96,256]{2,1,0:T(8,128)(2,1)}, bf16[3,96,256]{2,1,0:T(8,128)(2,1)S(1)}, u32[]{:S(2)}) copy-start(bf16[3,96,256]{2,1,0:T(8,128)(2,1)S(1)} %collective-permute-done.16.refs_3_) | copy-start | bytes 442372
  341.1 6.1 %collective-permute-start.18 = (bf16[3,96,256]{2,1,0:T(8,128)(2,1)S(1)}, bf16[3,96,256]{2,1,0:T(8,128)(2,1)S(1)}, u32[]{:S(2)}, u32[]{:S(2)}) collective-permute-start(bf16[3,96,256]{2,1,0:T(8,128)(2,1)S(1)} %copy-done.25), channel_id=1, source_target_pairs={{0,160},{32,192},{64,224},{96,0},{128,32},{160,64},{192,96},{224,1... | collective-permute-start | bytes 442376 | tf_op jit(solution)/shard_map/ppermute | solution.py:351
  343.6 8.2 %copy-start.17 = (bf16[3,96,256]{2,1,0:T(8,128)(2,1)}, bf16[3,96,256]{2,1,0:T(8,128)(2,1)S(1)}, u32[]{:S(2)}) copy-start(bf16[3,96,256]{2,1,0:T(8,128)(2,1)S(1)} %collective-permute-done.17.refs_4_) | copy-start | bytes 442372
  343.6 6.3 %collective-permute-start.19 = (bf16[3,96,256]{2,1,0:T(8,128)(2,1)S(1)}, bf16[3,96,256]{2,1,0:T(8,128)(2,1)S(1)}, u32[]{:S(2)}, u32[]{:S(2)}) collective-permute-start(bf16[3,96,256]{2,1,0:T(8,128)(2,1)S(1)} %copy-done.24), channel_id=1, source_target_pairs={{0,192},{32,224},{64,0},{96,32},{128,64},{160,96},{192,128},{224,1... | collective-permute-start | bytes 442376 | tf_op jit(solution)/shard_map/ppermute | solution.py:351
  347.2 4.6 %copy-start.18 = (bf16[3,96,256]{2,1,0:T(8,128)(2,1)}, bf16[3,96,256]{2,1,0:T(8,128)(2,1)S(1)}, u32[]{:S(2)}) copy-start(bf16[3,96,256]{2,1,0:T(8,128)(2,1)S(1)} %collective-permute-done.18.refs_5_) | copy-start | bytes 442372
  347.2 4.6 %collective-permute-start.20 = (bf16[3,96,256]{2,1,0:T(8,128)(2,1)S(1)}, bf16[3,96,256]{2,1,0:T(8,128)(2,1)S(1)}, u32[]{:S(2)}, u32[]{:S(2)}) collective-permute-start(bf16[3,96,256]{2,1,0:T(8,128)(2,1)S(1)} %copy-done.23), channel_id=1, source_target_pairs={{0,224},{32,0},{64,32},{96,64},{128,96},{160,128},{192,160},{224,1... | collective-permute-start | bytes 442376 | tf_op jit(solution)/shard_map/ppermute | solution.py:351
  349.8 2.0 copy-start.19
  351.8 0.7 copy-start.20
